TPU v7x, 32 devices: a whole 2x2x4 slice. The times are simulated.
32 devices in a mesh: win: 8 (over z, x), frm: 4 (over y, core).
Axes of the slice: x: 2, y: 2, z: 4, core: 2. Of those that a mesh axis runs over, the one named last changes fastest.
Arguments:
- hidden_state: bfloat16 [8192, 1536], P(('win', 'frm')), may hold values from -600 to 600
- latent: float32 [8192, 64], P(('win', 'frm')), may hold values from -6 to 6
- stale_kv: bfloat16 [8192, 1536], P(('win', 'frm')), may hold values from -100 to 100
- mod_shift: float32 [8, 1536], P('win'), may hold values from -3 to 3
- mod_scale: float32 [8, 1536], P('win'), may hold values from -3 to 3
- mod_gate: float32 [8, 1536], P('win'), may hold values from 0.5 to 4
- w_query: bfloat16 [1536, 768], replicated, may hold values from -0.29882812 to 0.29882812
- w_keyval: bfloat16 [1536, 1536], replicated, may hold values from -0.15625 to 0.15625
- w_out: bfloat16 [768, 1536], replicated, may hold values from -0.21875 to 0.21875
- w_final: bfloat16 [1536, 64], replicated, may hold values from -0.15625 to 0.15625
- step_size: float32 [8], P('win'), may hold values from 0.5 to 1.5
Outputs:
- next_latent: float32 [8192, 64], P(('win', 'frm'))
All inputs are finite; a program needn't handle non-finite values.
Results may differ from a plain program's by a relative error of at most 0.0024.
Values may be sent and summed in bfloat16 or wider, within the bound.
A program may use at most 192 MiB of HBM per device.

v0:
```python
import jax
import jax.numpy as jnp
from jax import lax
from jax.sharding import PartitionSpec as P

HEADS = 12
HEAD_DIM = 64


def from_behind(value, axis, by):
    devices = lax.axis_size(axis)
    return lax.ppermute(value, axis, [(i, (i + by) % devices) for i in range(devices)])


def from_behind_2(block, axis, distance):
    devices = range(lax.axis_size(axis))
    route = [(i - distance, i) for i in devices if i - distance in devices]
    return lax.ppermute(block, axis, route)


def layer_norm(values):
    average = jnp.mean(values, axis=-1, keepdims=True)
    centred = values - average
    variance = jnp.mean(centred * centred, axis=-1, keepdims=True)
    return centred * lax.rsqrt(variance + 1e-06)


def on_device(
    hidden_state,
    latent,
    stale_kv,
    mod_shift,
    mod_scale,
    mod_gate,
    w_query,
    w_keyval,
    w_out,
    w_final,
    step_size,
):
    local_rows = hidden_state.shape[0]
    query_width = HEADS * HEAD_DIM
    scale_factor = HEAD_DIM ** (-0.5)
    stream = hidden_state.astype(jnp.float32)
    modulated = (layer_norm(stream) * (1.0 + mod_scale) + mod_shift).astype(jnp.bfloat16)
    queries = jnp.dot(modulated, w_query, preferred_element_type=jnp.float32).astype(jnp.bfloat16)
    fresh_kv = jnp.dot(modulated, w_keyval, preferred_element_type=jnp.float32).astype(jnp.bfloat16)
    query_heads = queries.reshape(local_rows, HEADS, HEAD_DIM)
    own_start = lax.axis_index("frm") * local_rows
    gathered = lax.all_gather(stale_kv, "frm", axis=0, tiled=True)
    merged_kv = lax.dynamic_update_slice_in_dim(gathered, fresh_kv, own_start, 0)
    maxima = jnp.full((HEADS, local_rows), -1e30, jnp.float32)
    piece_rows = merged_kv.shape[0]
    key_rows = merged_kv[:, :query_width].reshape(piece_rows, HEADS, HEAD_DIM)
    value_rows = merged_kv[:, query_width:].reshape(piece_rows, HEADS, HEAD_DIM)
    new_maxima = []
    new_totals = []
    new_running = []
    for first_head in range(0, HEADS, 4):
        head_span = slice(first_head, first_head + 4)
        scores = (
            jnp.einsum(
                "qhd,khd->hqk",
                query_heads[:, head_span],
                key_rows[:, head_span],
                preferred_element_type=jnp.float32,
            )
            * scale_factor
        )
        old_max = maxima[head_span]
        new_max = jnp.maximum(old_max, jnp.max(scores, axis=-1))
        probs = jnp.exp(scores - new_max[:, :, None])
        new_totals.append(jnp.sum(probs, axis=-1))
        summed = jnp.einsum(
            "hqk,khd->qhd",
            probs.astype(jnp.bfloat16),
            value_rows[:, head_span],
            preferred_element_type=jnp.float32,
        )
        new_running.append(summed)
        new_maxima.append(new_max)
    attended = (
        jnp.concatenate(new_running, axis=1)
        / jnp.transpose(jnp.concatenate(new_totals, axis=0))[:, :, None]
    )
    attention = attended.reshape(local_rows, query_width).astype(jnp.bfloat16)
    combined = stream + mod_gate * jnp.dot(attention, w_out, preferred_element_type=jnp.float32)
    normed = layer_norm(combined).astype(jnp.bfloat16)
    velocity = jnp.dot(normed, w_final, preferred_element_type=jnp.float32)
    advanced = latent + step_size[0] * velocity
    frame_devs = lax.axis_size("frm")
    window_devs = lax.axis_size("win")
    half_devs = frame_devs // 2
    frame_id = lax.axis_index("frm")
    window_id = lax.axis_index("win")
    turned = from_behind(advanced, "frm", half_devs)
    from_before = from_behind_2(turned, "win", 1)
    from_after = from_behind_2(turned, "win", -1)
    window_frames = local_rows * frame_devs
    seam_frames = window_frames // 2
    frame_pos = (frame_id * local_rows + jnp.arange(local_rows, dtype=jnp.int32)).astype(
        jnp.float32
    )[:, None]
    head_ramp = (frame_pos + 0.5) / seam_frames
    in_head = (frame_pos < seam_frames) & (window_id > 0)
    tail_ramp = (frame_pos - (window_frames - seam_frames) + 0.5) / seam_frames
    in_tail = (frame_pos >= window_frames - seam_frames) & (window_id < window_devs - 1)
    blended = jnp.where(in_head, (1.0 - head_ramp) * from_before + head_ramp * advanced, advanced)
    blended = jnp.where(in_tail, (1.0 - tail_ramp) * advanced + tail_ramp * from_after, blended)
    return blended


def solution(mesh):
    placed = (
        P(("win", "frm"), None),
        P(("win", "frm"), None),
        P(("win", "frm"), None),
        P("win", None),
        P("win", None),
        P("win", None),
        P(),
        P(),
        P(),
        P(),
        P("win"),
    )
    return jax.shard_map(
        on_device, mesh=mesh, in_specs=placed, out_specs=P(("win", "frm"), None), check_vma=False
    )
```

profile of v0, /device:TPU:0, one launch (start us, length us, event | category | flops | bytes accessed | tf_op | source)
XLA Modules:
  0.0 98.3 jit_solution(14476462986288637852)
XLA Ops:
  8.7 0.7 reduce
  10.1 1.3 %convert_reduce_fusion = f32[256]{0:T(256)S(1)} fusion(bf16[256,1536]{1,0:T(8,128)(2,1)} %param.11), kind=kLoop, calls=%fused_computation.17 | loop fusion | flops 786176 | bytes 787456 | tf_op jit(solution)/shard_map/reduce_sum | solution.py:22
  11.4 1.5 %fusion.22 = f32[256]{0:T(256)S(1)} fusion(bf16[256,1536]{1,0:T(8,128)(2,1)} %param.11, f32[256]{0:T(256)S(1)} %broadcast_multiply_fusion.1), kind=kLoop, calls=%fused_computation.29 | loop fusion | flops 1572608 | bytes 788480 | tf_op jit(solution)/shard_map/reduce_sum | solution.py:24
  13.5 3.3 %convolution_convert_fusion.1 = bf16[256,768]{1,0:T(8,128)(2,1)} fusion(bf16[1536,768]{1,0:T(8,128)(2,1)} %param.17, bf16[256,1536]{1,0:T(8,128)(2,1)S(1)} %copy-done.1, f32[1536]{0:T(1024)S(1)} %reduce.2, f32[1536]{0:T(1024)S(1)} %add_reduce_fusion, f32[256]{0:T(256)S(1)} %add_rsqrt_fusion.1, f32[256]{0:T(256)S(1)} %broadcast_multiply_fusion.1), kind=kOutput, calls=%fused_computation.35 | convolution fusion | flops 606535680 | bytes 3553280 | tf_op jit(solution)/shard_map/dot_general | solution.py:46
  16.8 1.2 %copy.18 = bf16[256,768]{0,1:T(8,128)(2,1)S(1)} copy(bf16[256,768]{1,0:T(8,128)(2,1)} %convolution_convert_fusion.1) | data formatting | bytes 786432 | tf_op jit(solution)/shard_map/convert_element_type | solution.py:46
  18.6 21.6 %all-gather.2.cloned.1.call-done = bf16[1024,1536]{1,0:T(8,128)(2,1)} async-done(((bf16[256,1536]{1,0:T(8,128)(2,1)}), bf16[1024,1536]{1,0:T(8,128)(2,1)}) %all-gather.2.cloned.1.call-update) | async-done | bytes 3145744 | tf_op jit(solution)/shard_map/all_gather | solution.py:50
  40.2 4.7 %fusion.7 = bf16[1024,1536]{1,0:T(8,128)(2,1)} fusion(bf16[1024,1536]{1,0:T(8,128)(2,1)} %all-gather.2.cloned.1.call-done, s32[]{:T(128)S(6)} %select_n.10, bf16[1536,1536]{1,0:T(8,128)(2,1)} %param.18, bf16[256,1536]{1,0:T(8,128)(2,1)S(1)} %copy-done.1, f32[1536]{0:T(1024)} %copy-done.9, f32[1536]{0:T(1024)S(1)} %add_reduce_fusion, f32[256]{0:T(256)} %copy-done.14, ...), kind=kOutput, calls=%fused_computation.15 | convolution fusion | flops 1210712064 | bytes 6307844 | tf_op jit(solution)/shard_map/dot_general | solution.py:47
  44.9 3.8 %fusion.50 = (bf16[1024,768]{1,0:T(8,128)(2,1)}, bf16[1024,768]{1,0:T(8,128)(2,1)}) fusion(bf16[1024,1536]{1,0:T(8,128)(2,1)} %fusion.7), kind=kLoop, calls=%fused_computation.71 | loop fusion | bytes 6291456 | tf_op jit(solution)/shard_map/slice | solution.py:54
  48.6 2.6 %copy.19 = bf16[1024,768]{0,1:T(8,128)(2,1)} copy(bf16[1024,768]{1,0:T(8,128)(2,1)} %get-tuple-element.5) | data formatting | bytes 3145728 | tf_op jit(solution)/shard_map/slice | solution.py:54
  51.3 4.4 %multiply_reduce_fusion = (f32[4,256]{1,0:T(4,128)}, f32[4,256,1024]{2,1,0:T(8,128)}) fusion(bf16[256,12,64]{0,2,1:T(8,128)(2,1)S(1)} %bitcast.32, bf16[1024,12,64]{0,2,1:T(8,128)(2,1)} %bitcast.28), kind=kOutput, calls=%fused_computation.3 | convolution fusion | flops 136313856 | bytes 5115904 | tf_op jit(solution)/shard_map/qhd,khd->hqk/dot_general | solution.py:62
  55.7 2.8 %multiply_reduce_fusion.1 = (f32[4,256]{1,0:T(4,128)S(1)}, f32[4,256,1024]{2,1,0:T(8,128)}) fusion(bf16[256,12,64]{0,2,1:T(8,128)(2,1)S(1)} %bitcast.33, bf16[1024,12,64]{0,2,1:T(8,128)(2,1)S(1)} %bitcast.29), kind=kOutput, calls=%fused_computation.4 | convolution fusion | flops 136313856 | bytes 5115904 | tf_op jit(solution)/shard_map/qhd,khd->hqk/dot_general | solution.py:62
  58.5 2.8 %multiply_reduce_fusion.2 = (f32[4,256]{1,0:T(4,128)S(1)}, f32[4,256,1024]{2,1,0:T(8,128)}) fusion(bf16[256,12,64]{0,2,1:T(8,128)(2,1)S(1)} %bitcast.34, bf16[1024,12,64]{0,2,1:T(8,128)(2,1)S(1)} %bitcast.30), kind=kOutput, calls=%fused_computation.5 | convolution fusion | flops 136313856 | bytes 5115904 | tf_op jit(solution)/shard_map/qhd,khd->hqk/dot_general | solution.py:62
  61.2 2.6 %copy.17 = bf16[1024,768]{0,1:T(8,128)(2,1)} copy(bf16[1024,768]{1,0:T(8,128)(2,1)} %get-tuple-element.6) | data formatting | bytes 3145728 | tf_op jit(solution)/shard_map/slice | solution.py:55
  63.9 3.2 %fusion.4 = f32[4,256]{1,0:T(4,128)S(1)} fusion(f32[4,256,1024]{2,1,0:T(8,128)} %get-tuple-element.8, f32[4,256]{1,0:T(4,128)S(1)} %broadcast_maximum_fusion), kind=kLoop, calls=%fused_computation.10 | loop fusion | flops 3144704 | bytes 4202496 | tf_op jit(solution)/shard_map/reduce_sum | solution.py:73
  67.3 2.1 %fusion.32 = f32[256,4,64]{0,2,1:T(8,128)S(1)} fusion(bf16[1024,12,64]{0,2,1:T(8,128)(2,1)} %bitcast.25, f32[4,256,1024]{2,1,0:T(8,128)S(1)} %copy-done.4, f32[4,256]{1,0:T(4,128)S(1)} %broadcast_maximum_fusion), kind=kOutput, calls=%fused_computation.38 | convolution fusion | flops 137363456 | bytes 6033408 | tf_op jit(solution)/shard_map/hqk,khd->qhd/dot_general | solution.py:74
  70.1 0.9 fusion.29
  71.1 1.3 %copy-done.3 = f32[4,256,1024]{2,1,0:T(8,128)S(1)} copy-done((f32[4,256,1024]{2,1,0:T(8,128)S(1)}, f32[4,256,1024]{2,1,0:T(8,128)}, u32[]{:S(2)}) %copy-start.3) | copy-done | bytes 4194328
  72.3 1.8 %fusion = (f32[4,256]{1,0:T(4,128)S(1)}, f32[4,256]{1,0:T(4,128)S(1)}) fusion(f32[4,256,1024]{2,1,0:T(8,128)S(1)} %copy-done.3, f32[4,256]{1,0:T(4,128)S(1)} %broadcast_maximum_fusion.2, f32[4,256]{1,0:T(4,128)S(1)} %broadcast_maximum_fusion.1, f32[4,256,1024]{2,1,0:T(8,128)S(1)} %copy-done.2), kind=kLoop, calls=%fused_computation.6 | loop fusion | flops 6289408 | bytes 8404992 | tf_op jit(solution)/shard_map/reduce_sum | solution.py:73
  74.1 0.9 fusion.26
  75.2 0.9 fusion.51
  77.3 3.9 %collective-permute-done = f32[256,64]{0,1:T(8,128)S(1)} collective-permute-done((f32[256,64]{0,1:T(8,128)S(1)}, f32[256,64]{0,1:T(8,128)S(1)}, u32[]{:S(2)}, u32[]{:S(2)}) %collective-permute-start) | collective-permute-done | bytes 65568 | tf_op jit(solution)/shard_map/ppermute | solution.py:12
  81.2 3.4 %collective-permute-start.2 = (f32[256,64]{0,1:T(8,128)S(1)}, f32[256,64]{0,1:T(8,128)S(1)}, u32[]{:S(2)}, u32[]{:S(2)}) collective-permute-start(f32[256,64]{0,1:T(8,128)S(1)} %collective-permute-done), channel_id=1, source_target_pairs={{0,4},{4,8},{8,12},{12,16},{16,20},{20,24},{24,28},{1,5},{5,9},{9,... | collective-permute-start | bytes 196616 | tf_op jit(solution)/shard_map/ppermute | solution.py:18
  84.6 1.3 %collective-permute-start.1 = (f32[256,64]{0,1:T(8,128)S(1)}, f32[256,64]{0,1:T(8,128)S(1)}, u32[]{:S(2)}, u32[]{:S(2)}) collective-permute-start(f32[256,64]{0,1:T(8,128)S(1)} %collective-permute-done), channel_id=1, source_target_pairs={{4,0},{8,4},{12,8},{16,12},{20,16},{24,20},{28,24},{5,1},{9,5},{13... | collective-permute-start | bytes 196616 | tf_op jit(solution)/shard_map/ppermute | solution.py:18
  86.5 4.3 %collective-permute-done.1 = f32[256,64]{0,1:T(8,128)S(1)} collective-permute-done((f32[256,64]{0,1:T(8,128)S(1)}, f32[256,64]{0,1:T(8,128)S(1)}, u32[]{:S(2)}, u32[]{:S(2)}) %collective-permute-start.1) | collective-permute-done | bytes 65568 | tf_op jit(solution)/shard_map/ppermute | solution.py:18
  (50 shorter events, 6.7 us)
Async XLA Ops:
  6.5 68.6 %copy-start = (bf16[768,1536]{1,0:T(8,128)(2,1)S(1)}, bf16[768,1536]{1,0:T(8,128)(2,1)}, u32[]{:S(2)}) copy-start(bf16[768,1536]{1,0:T(8,128)(2,1)} %param.19) | copy-start | bytes 7077892
  6.5 6.9 %copy-start.1 = (bf16[256,1536]{1,0:T(8,128)(2,1)S(1)}, bf16[256,1536]{1,0:T(8,128)(2,1)}, u32[]{:S(2)}) copy-start(bf16[256,1536]{1,0:T(8,128)(2,1)} %param.11) | copy-start | bytes 2359300
  6.5 33.6 %all-gather.2.cloned.1.call-start = ((), (), s32[]{:S(2)}) async-start(), calls=%async_computation | async-start | bytes 3932160 | tf_op jit(solution)/shard_map/all_gather | solution.py:50
  8.7 4.3 %copy-start.9 = (f32[1536]{0:T(1024)}, f32[1536]{0:T(1024)S(1)}, u32[]{:S(2)}) copy-start(f32[1536]{0:T(1024)S(1)} %reduce.2) | copy-start | bytes 18436
  11.4 1.5 %copy-start.12 = (f32[256]{0:T(256)}, f32[256]{0:T(256)S(1)}, u32[]{:S(2)}) copy-start(f32[256]{0:T(256)S(1)} %broadcast_multiply_fusion.1) | copy-start | bytes 3076
  13.0 0.5 copy-start.14
  51.3 4.5 %copy-start.6 = (bf16[1024,768]{0,1:T(8,128)(2,1)S(1)}, bf16[1024,768]{0,1:T(8,128)(2,1)}, u32[]{:S(2)}) copy-start(bf16[1024,768]{0,1:T(8,128)(2,1)} %copy.19) | copy-start | bytes 4718596
  61.2 2.6 %copy-start.13 = (f32[4,256]{1,0:T(4,128)S(1)}, f32[4,256]{1,0:T(4,128)}, u32[]{:S(2)}) copy-start(f32[4,256]{1,0:T(4,128)} %get-tuple-element.7) | copy-start | bytes 12292
  63.9 3.4 %copy-start.4 = (f32[4,256,1024]{2,1,0:T(8,128)S(1)}, f32[4,256,1024]{2,1,0:T(8,128)}, u32[]{:S(2)}) copy-start(f32[4,256,1024]{2,1,0:T(8,128)} %get-tuple-element.8) | copy-start | bytes 12582916
  67.3 2.3 %copy-start.2 = (f32[4,256,1024]{2,1,0:T(8,128)S(1)}, f32[4,256,1024]{2,1,0:T(8,128)}, u32[]{:S(2)}) copy-start(f32[4,256,1024]{2,1,0:T(8,128)} %get-tuple-element.10) | copy-start | bytes 12582916
  67.3 2.8 %copy-start.5 = (bf16[1024,768]{0,1:T(8,128)(2,1)S(1)}, bf16[1024,768]{0,1:T(8,128)(2,1)}, u32[]{:S(2)}) copy-start(bf16[1024,768]{0,1:T(8,128)(2,1)} %copy.17) | copy-start | bytes 4718596
  70.1 2.2 %copy-start.3 = (f32[4,256,1024]{2,1,0:T(8,128)S(1)}, f32[4,256,1024]{2,1,0:T(8,128)}, u32[]{:S(2)}) copy-start(f32[4,256,1024]{2,1,0:T(8,128)} %get-tuple-element.12) | copy-start | bytes 12582916
  75.2 1.2 %copy-start.7 = (bf16[1536,64]{0,1:T(8,128)(2,1)S(1)}, bf16[1536,64]{0,1:T(8,128)(2,1)}, u32[]{:S(2)}) copy-start(bf16[1536,64]{0,1:T(8,128)(2,1)} %param.20) | copy-start | bytes 589828
  75.2 1.2 %copy-start.8 = (f32[256,64]{0,1:T(8,128)S(1)}, f32[256,64]{0,1:T(8,128)}, u32[]{:S(2)}) copy-start(f32[256,64]{0,1:T(8,128)} %param.12) | copy-start | bytes 196612
  76.1 14.7 %copy-start.10 = (f32[256]{0:T(256)S(1)}, f32[256]{0:T(256)}, u32[]{:S(2)}) copy-start(f32[256]{0:T(256)} %get-tuple-element.17) | copy-start | bytes 3076
  76.1 14.7 %copy-start.11 = (f32[256]{0:T(256)S(1)}, f32[256]{0:T(256)}, u32[]{:S(2)}) copy-start(f32[256]{0:T(256)} %get-tuple-element.18) | copy-start | bytes 3076
  76.9 4.3 %collective-permute-start = (f32[256,64]{0,1:T(8,128)S(1)}, f32[256,64]{0,1:T(8,128)S(1)}, u32[]{:S(2)}, u32[]{:S(2)}) collective-permute-start(f32[256,64]{0,1:T(8,128)S(1)} %fusion.35), channel_id=1, source_target_pairs={{0,2},{1,3},{2,0},{3,1},{4,6},{5,7},{6,4},{7,5},{8,10},{9,11},{10,... | collective-permute-start | bytes 196616 | tf_op jit(solution)/shard_map/ppermute | solution.py:12
  81.2 5.3 %collective-permute-start.2 = (f32[256,64]{0,1:T(8,128)S(1)}, f32[256,64]{0,1:T(8,128)S(1)}, u32[]{:S(2)}, u32[]{:S(2)}) collective-permute-start(f32[256,64]{0,1:T(8,128)S(1)} %collective-permute-done), channel_id=1, source_target_pairs={{0,4},{4,8},{8,12},{12,16},{16,20},{20,24},{24,28},{1,5},{5,9},{9,... | collective-permute-start | bytes 196616 | tf_op jit(solution)/shard_map/ppermute | solution.py:18
  84.6 6.2 %collective-permute-start.1 = (f32[256,64]{0,1:T(8,128)S(1)}, f32[256,64]{0,1:T(8,128)S(1)}, u32[]{:S(2)}, u32[]{:S(2)}) collective-permute-start(f32[256,64]{0,1:T(8,128)S(1)} %collective-permute-done), channel_id=1, source_target_pairs={{4,0},{8,4},{12,8},{16,12},{20,16},{24,20},{28,24},{5,1},{9,5},{13... | collective-permute-start | bytes 196616 | tf_op jit(solution)/shard_map/ppermute | solution.py:18
Sparse Core Ops, SparseCore 0:
  8.9 31.2 all-gather.1
where the time goes:
time: 98.8 us; the launch traced here: 98.3 us
  waiting for transfers between devices  31.1 us (31%)
  matrix products  23.2 us (23%)
  between operations  14.3 us (14%)
  local copies, waits for them, and re-layouts  12.9 us (13%)
  other arithmetic  11.7 us (12%)
  starting transfers between devices  5.05 us (5%)
    all_gather x1, waiting for transfers between devices, on_device(): gathered = lax.all_gather(stale_kv, 'frm', axis=0, tiled=True)  21.6 us
    dot_general x3, matrix products, on_device(): jnp.einsum('qhd,khd->hqk', query_heads[:, head_span], key_rows[:, head_sp...  9.97 us
    slice x2, local copies, waits for them, and re-layouts, on_device(): key_rows = merged_kv[:, :query_width].reshape(piece_rows, HEADS, HEAD_DIM)  6.41 us
    reduce_sum x2, other arithmetic, on_device(): new_totals.append(jnp.sum(probs, axis=-1))  5.01 us
    ppermute x2, waiting for transfers between devices, from_behind_2(): return lax.ppermute(block, axis, route)  4.84 us
    dot_general x1, matrix products, on_device(): jnp.dot(modulated, w_keyval, preferred_element_type=jnp.float32)  4.67 us
    ppermute x2, starting transfers between devices, from_behind_2(): return lax.ppermute(block, axis, route)  4.66 us
    dot_general x3, matrix products, on_device(): jnp.einsum('hqk,khd->qhd', probs.astype(jnp.bfloat16), value_rows[:, head...  3.95 us
  transfers between devices with their start and end apart: 4, of which 4 were waited for; matrix products, arithmetic and copies ran while one was open for 10% of the time, Pallas kernels for 0%

commit v1 on v0

v1 whole, which is shorter than its diff:
```python
import functools

import jax
import jax.numpy as jnp
from jax import lax
from jax.experimental import pallas as pl
from jax.experimental.pallas import tpu as pltpu
from jax.sharding import PartitionSpec as P

HEAD_DIM = 64
PAIR = 2 * HEAD_DIM
TILE = 256
LN_ROWS = 32
MESH = pl.DeviceIdType.MESH
NT = (((1,), (1,)), ((), ()))


def layer_norm(values):
    average = jnp.mean(values, axis=-1, keepdims=True)
    centred = values - average
    variance = jnp.mean(centred * centred, axis=-1, keepdims=True)
    return centred * lax.rsqrt(variance + 1e-06)


def kernel(
    windows,
    frame_devs,
    step_ref,
    hidden_hbm,
    latent_hbm,
    stale_hbm,
    shift_hbm,
    scale_hbm,
    gate_hbm,
    wq_hbm,
    wkv_hbm,
    wo_hbm,
    wf_hbm,
    out_ref,
    hidden,
    latent,
    shift,
    scale,
    gate,
    wq,
    wkv,
    wo,
    wf,
    modulated,
    queries,
    kv,
    attention,
    combined,
    normed,
    advanced,
    other,
    load_sem,
    send_sem,
    recv_sem,
    seam_send,
    seam_recv,
):
    rows, width = hidden.shape
    qw = queries.shape[1]
    pairs = qw // PAIR
    chips = frame_devs // 2
    half_devs = frame_devs // 2
    w = lax.axis_index("win")
    f = lax.axis_index("frm")
    chip, core = f // 2, f % 2
    sibling = (w, chip * 2 + (1 - core))
    peers = [(w, ((chip + j) % chips) * 2 + core) for j in range(1, chips)]
    in_tail = f >= half_devs
    has_partner = jnp.where(in_tail, w < windows - 1, w > 0)
    partner = (
        jnp.where(in_tail, w + 1, w - 1),
        jnp.where(in_tail, f - half_devs, f + half_devs),
    )

    loads = [
        pltpu.make_async_copy(src, dst, load_sem.at[i])
        for i, (src, dst) in enumerate(
            [
                (hidden_hbm, hidden),
                (scale_hbm, scale),
                (shift_hbm, shift),
                (wq_hbm, wq),
                (wkv_hbm.at[:, pl.ds(0, qw)], wkv.at[:, pl.ds(0, qw)]),
                (wkv_hbm.at[:, pl.ds(qw, qw)], wkv.at[:, pl.ds(qw, qw)]),
                (gate_hbm, gate),
                (wo_hbm, wo),
                (wf_hbm, wf),
                (latent_hbm, latent),
            ]
        )
    ]
    for load in loads:
        load.start()

    barrier = pltpu.get_barrier_semaphore()
    for device in [sibling] + peers:
        pl.semaphore_signal(barrier, inc=1, device_id=device, device_id_type=MESH)

    @pl.when(has_partner)
    def _():
        pl.semaphore_signal(barrier, inc=1, device_id=partner, device_id_type=MESH)

    pl.semaphore_wait(barrier, jnp.where(has_partner, chips + 1, chips))

    def columns(g, part):
        return pl.ds(pl.multiple_of(part * qw + g * PAIR, PAIR), PAIR)

    def send(source, slot, device, g, part):
        return pltpu.make_async_remote_copy(
            src_ref=source.at[:, columns(g, part)],
            dst_ref=kv.at[pl.ds(slot * rows, rows), columns(g, part)],
            send_sem=send_sem.at[slot, g, part],
            recv_sem=recv_sem.at[slot, g, part],
            device_id=device,
            device_id_type=MESH,
        )

    def to_sibling(g, part):
        return send(stale_hbm, 1, sibling, g, part)

    def to_peer(j, g, part):
        return send(stale_hbm, 2 * j, peers[j - 1], g, part)

    def forward(j, g, part):
        return send(kv.at[pl.ds(2 * j * rows, rows)], 2 * j + 1, sibling, g, part)

    @pl.loop(0, pairs)
    def _(g):
        for part in range(2):
            for j in range(1, chips):
                to_peer(j, g, part).start()
            to_sibling(g, part).start()

    def arrive(g):
        for j in range(1, chips):
            for part in range(2):
                to_peer(j, g, part).wait_recv()
                forward(j, g, part).start()

    def ready(g):
        for part in range(2):
            to_sibling(g, part).wait_recv()
            for j in range(1, chips):
                forward(j, g, part).wait_recv()

    for load in loads[:3]:
        load.wait()

    @pl.loop(0, rows // LN_ROWS)
    def _(i):
        at = pl.ds(pl.multiple_of(i * LN_ROWS, LN_ROWS), LN_ROWS)
        line = layer_norm(hidden[at, :].astype(jnp.float32))
        modulated[at, :] = (line * (1.0 + scale[...]) + shift[...]).astype(jnp.bfloat16)

    loads[3].wait()

    @pl.loop(0, qw // TILE)
    def _(i):
        at = pl.ds(pl.multiple_of(i * TILE, TILE), TILE)
        tile = jnp.dot(modulated[...], wq[:, at], preferred_element_type=jnp.float32)
        queries[:, at] = (tile * HEAD_DIM ** (-0.5)).astype(jnp.bfloat16)

    loads[4].wait()
    loads[5].wait()

    @pl.loop(0, 2 * qw // TILE)
    def _(i):
        at = pl.ds(pl.multiple_of(i * TILE, TILE), TILE)
        tile = jnp.dot(modulated[...], wkv[:, at], preferred_element_type=jnp.float32)
        kv[pl.ds(0, rows), at] = tile.astype(jnp.bfloat16)

    def attend(g):
        query = queries[:, columns(g, 0)]
        keys = kv[:, columns(g, 0)]
        values = kv[:, columns(g, 1)]
        low = lax.broadcasted_iota(jnp.int32, (rows, PAIR), 1) < HEAD_DIM
        heads = []
        for head in range(2):
            chosen = low if head == 0 else jnp.logical_not(low)
            masked = jnp.where(chosen, query.astype(jnp.float32), 0.0).astype(jnp.bfloat16)
            scores = lax.dot_general(masked, keys, NT, preferred_element_type=jnp.float32)
            probs = jnp.exp(scores - jnp.max(scores, axis=-1, keepdims=True))
            totals = jnp.sum(probs, axis=-1, keepdims=True)
            summed = jnp.dot(
                probs.astype(jnp.bfloat16), values, preferred_element_type=jnp.float32
            )
            heads.append(summed / totals)
        attention[:, columns(g, 0)] = jnp.where(low, heads[0], heads[1]).astype(jnp.bfloat16)

    arrive(0)
    last = TILE // PAIR
    early = qw - TILE

    @pl.loop(0, pairs - last)
    def _(g):
        arrive(g + 1)
        ready(g)
        attend(g)

    for load in loads[6:]:
        load.wait()

    @pl.loop(0, width // TILE)
    def _(i):
        at = pl.ds(pl.multiple_of(i * TILE, TILE), TILE)
        tile = jnp.dot(
            attention[:, pl.ds(0, early)], wo[pl.ds(0, early), at],
            preferred_element_type=jnp.float32,
        )
        combined[:, at] = hidden[:, at].astype(jnp.float32) + gate[:, at] * tile

    for g in range(pairs - last, pairs):
        if g + 1 < pairs:
            arrive(g + 1)
        ready(g)
        attend(g)

    for i in range(width // TILE):
        at = pl.ds(i * TILE, TILE)
        tile = jnp.dot(
            attention[:, pl.ds(early, TILE)], wo[pl.ds(early, TILE), at],
            preferred_element_type=jnp.float32,
        )
        combined[:, at] += gate[:, at] * tile

    @pl.loop(0, rows // LN_ROWS)
    def _(i):
        at = pl.ds(pl.multiple_of(i * LN_ROWS, LN_ROWS), LN_ROWS)
        normed[at, :] = layer_norm(combined[at, :]).astype(jnp.bfloat16)

    velocity = lax.dot_general(wf[...], normed[...], NT, preferred_element_type=jnp.float32)
    advanced[...] = latent[...] + step_ref[0] * velocity

    seam = pltpu.make_async_remote_copy(
        src_ref=advanced,
        dst_ref=other,
        send_sem=seam_send,
        recv_sem=seam_recv,
        device_id=partner,
        device_id_type=MESH,
    )

    @pl.when(has_partner)
    def _():
        seam.start()

    @pl.loop(0, pairs)
    def _(g):
        for part in range(2):
            to_sibling(g, part).wait_send()
            for j in range(1, chips):
                to_peer(j, g, part).wait_send()
                forward(j, g, part).wait_send()

    @pl.when(has_partner)
    def _():
        seam_frames = half_devs * rows
        first = jnp.where(in_tail, f - half_devs, f) * rows
        place = first + lax.broadcasted_iota(jnp.int32, advanced.shape, 1)
        ramp = (place.astype(jnp.float32) + 0.5) / seam_frames
        own = jnp.where(in_tail, 1.0 - ramp, ramp)
        seam.wait()
        out_ref[...] = own * advanced[...] + (1.0 - own) * other[...]

    @pl.when(jnp.logical_not(has_partner))
    def _():
        out_ref[...] = advanced[...]


def on_device(
    windows,
    frame_devs,
    hidden_state,
    latent,
    stale_kv,
    mod_shift,
    mod_scale,
    mod_gate,
    w_query,
    w_keyval,
    w_out,
    w_final,
    step_size,
):
    rows, width = hidden_state.shape
    channels = latent.shape[1]
    qw = w_query.shape[1]
    pairs = qw // PAIR
    bf16, f32 = jnp.bfloat16, jnp.float32
    anywhere = pl.BlockSpec(memory_space=pl.ANY)
    result = pl.pallas_call(
        functools.partial(kernel, windows, frame_devs),
        out_shape=jax.ShapeDtypeStruct((channels, rows), f32),
        in_specs=[pl.BlockSpec(memory_space=pltpu.SMEM)] + [anywhere] * 10,
        out_specs=pl.BlockSpec(memory_space=pltpu.VMEM),
        scratch_shapes=[
            pltpu.VMEM((rows, width), bf16),
            pltpu.VMEM((channels, rows), f32),
            pltpu.VMEM((1, width), f32),
            pltpu.VMEM((1, width), f32),
            pltpu.VMEM((1, width), f32),
            pltpu.VMEM(w_query.shape, bf16),
            pltpu.VMEM(w_keyval.shape, bf16),
            pltpu.VMEM(w_out.shape, bf16),
            pltpu.VMEM((channels, width), bf16),
            pltpu.VMEM((rows, width), bf16),
            pltpu.VMEM((rows, qw), bf16),
            pltpu.VMEM((frame_devs * rows, 2 * qw), bf16),
            pltpu.VMEM((rows, qw), bf16),
            pltpu.VMEM((rows, width), f32),
            pltpu.VMEM((rows, width), bf16),
            pltpu.VMEM((channels, rows), f32),
            pltpu.VMEM((channels, rows), f32),
            pltpu.SemaphoreType.DMA((10,)),
            pltpu.SemaphoreType.DMA((frame_devs, pairs, 2)),
            pltpu.SemaphoreType.DMA((frame_devs, pairs, 2)),
            pltpu.SemaphoreType.DMA,
            pltpu.SemaphoreType.DMA,
        ],
        compiler_params=pltpu.CompilerParams(
            collective_id=0, has_side_effects=True, vmem_limit_bytes=56 * 1024 * 1024
        ),
        name="dit_window_step",
    )(
        step_size,
        hidden_state,
        latent.T,
        stale_kv,
        mod_shift,
        mod_scale,
        mod_gate,
        w_query,
        w_keyval,
        w_out,
        w_final.T,
    )
    return result.T


def solution(mesh):
    placed = (
        P(("win", "frm"), None),
        P(("win", "frm"), None),
        P(("win", "frm"), None),
        P("win", None),
        P("win", None),
        P("win", None),
        P(),
        P(),
        P(),
        P(),
        P("win"),
    )
    return jax.shard_map(
        functools.partial(on_device, mesh.shape["win"], mesh.shape["frm"]),
        mesh=mesh,
        in_specs=placed,
        out_specs=P(("win", "frm"), None),
        check_vma=False,
    )
```

time: 98.8 us -> 33.8 us (0.34)
  the two profiles are of different devices: /device:TPU:0 before, /device:TPU:21 now
where the time goes in v1:
time: 33.8 us; the launch traced here: 33.4 us
  Pallas kernels  31.3 us (93%)
  local copies, waits for them, and re-layouts  1.47 us (4%)
  between operations  0.66 us (2%)
    pallas_call x1, Pallas kernels, on_device(): pl.pallas_call(functools.partial(kernel, windows, frame_devs), out_shape=...  31.3 us
    unnamed x1, local copies, waits for them, and re-layouts  1.47 us

profile of v1, /device:TPU:21, one launch (start us, length us, event | category | flops | bytes accessed | tf_op | source)
XLA Modules:
  0.0 33.4 jit_solution(9895547280714030086)
XLA Ops:
  0.7 31.3 %dit_window_step.1 = f32[64,256]{1,0:T(8,128)} custom-call(f32[1]{0:T(128)S(6)} %copy.13.step_ref, bf16[256,1536]{1,0:T(8,128)(2,1)} %hidden_hbm.1, f32[64,256]{1,0:T(8,128)} %bitcast.5, bf16[256,1536]{1,0:T(8,128)(2,1)} %stale_hbm.1, f32[1,1536]{1,0:T(1,128)} %shift_hbm.1, f32[1,1536]{1,0:T(1,128)} %scale_hbm.1, f32[1,1536]{1,0:T(1,128)} %gate_hbm.1, ...), custom_call_target="tpu_custom_call" | custom-call | tf_op jit(solution)/shard_map/dit_window_step/pallas_call | solution.py:296
  32.0 1.5 %copy.14 = f32[256,64]{0,1:T(8,128)} copy(f32[256,64]{0,1:T(8,128)} %bitcast.3) | data formatting | bytes 131072

commit v2 on v1

--- a/solution.py
+++ b/solution.py
@@ -25,7 +25,7 @@
 def kernel(
     windows,
     frame_devs,
-    step_ref,
+    step_hbm,
     hidden_hbm,
     latent_hbm,
     stale_hbm,
@@ -36,7 +36,9 @@
     wkv_hbm,
     wo_hbm,
     wf_hbm,
-    out_ref,
+    advanced_hbm,
+    other_hbm,
+    step,
     hidden,
     latent,
     shift,
@@ -50,10 +52,12 @@
     queries,
     kv,
     attention,
+    maxima,
+    totals,
+    running,
     combined,
     normed,
     advanced,
-    other,
     load_sem,
     send_sem,
     recv_sem,
@@ -91,6 +95,7 @@
                 (wo_hbm, wo),
                 (wf_hbm, wf),
                 (latent_hbm, latent),
+                (step_hbm, step),
             ]
         )
     ]
@@ -142,12 +147,6 @@
                 to_peer(j, g, part).wait_recv()
                 forward(j, g, part).start()
 
-    def ready(g):
-        for part in range(2):
-            to_sibling(g, part).wait_recv()
-            for j in range(1, chips):
-                forward(j, g, part).wait_recv()
-
     for load in loads[:3]:
         load.wait()
 
@@ -174,33 +173,66 @@
         tile = jnp.dot(modulated[...], wkv[:, at], preferred_element_type=jnp.float32)
         kv[pl.ds(0, rows), at] = tile.astype(jnp.bfloat16)
 
-    def attend(g):
-        query = queries[:, columns(g, 0)]
-        keys = kv[:, columns(g, 0)]
-        values = kv[:, columns(g, 1)]
-        low = lax.broadcasted_iota(jnp.int32, (rows, PAIR), 1) < HEAD_DIM
+    low = lax.broadcasted_iota(jnp.int32, (rows, PAIR), 1) < HEAD_DIM
+
+    def attend(g, slot, slots, first, final):
+        at = columns(g, 0)
+        held = pl.ds(slot * rows, slots * rows)
+        query = queries[:, at].astype(jnp.float32)
+        keys, values = kv[held, at], kv[held, columns(g, 1)]
         heads = []
-        for head in range(2):
-            chosen = low if head == 0 else jnp.logical_not(low)
-            masked = jnp.where(chosen, query.astype(jnp.float32), 0.0).astype(jnp.bfloat16)
+        for chosen in (low, jnp.logical_not(low)):
+            masked = jnp.where(chosen, query, 0.0).astype(jnp.bfloat16)
             scores = lax.dot_general(masked, keys, NT, preferred_element_type=jnp.float32)
-            probs = jnp.exp(scores - jnp.max(scores, axis=-1, keepdims=True))
-            totals = jnp.sum(probs, axis=-1, keepdims=True)
+            top = jnp.max(scores, axis=-1, keepdims=True)
+            probs = jnp.exp(scores - top)
+            total = jnp.sum(probs, axis=-1, keepdims=True)
             summed = jnp.dot(
                 probs.astype(jnp.bfloat16), values, preferred_element_type=jnp.float32
             )
-            heads.append(summed / totals)
-        attention[:, columns(g, 0)] = jnp.where(low, heads[0], heads[1]).astype(jnp.bfloat16)
+            heads.append((top, total, summed))
+        top, total, summed = (jnp.where(low, *both) for both in zip(*heads))
+        if not first:
+            peak = jnp.maximum(maxima[:, at], top)
+            keep, add = jnp.exp(maxima[:, at] - peak), jnp.exp(top - peak)
+            top = peak
+            total = totals[:, at] * keep + total * add
+            summed = running[:, at] * keep + summed * add
+        if final:
+            attention[:, at] = (summed / total).astype(jnp.bfloat16)
+        else:
+            maxima[:, at], totals[:, at], running[:, at] = top, total, summed
+
+    def attend_local(start, stop):
+        @pl.loop(start, stop)
+        def _(g):
+            for part in range(2):
+                to_sibling(g, part).wait_recv()
+            attend(g, 0, 2, True, chips == 1)
+
+    def attend_remote(g):
+        for j in range(1, chips):
+            attend(g, 2 * j, 1, False, False)
+            for part in range(2):
+                forward(j, g, part).wait_recv()
+            attend(g, 2 * j + 1, 1, False, j == chips - 1)
 
     arrive(0)
+    attend_local(0, pairs // 2)
+    arrive(1)
+    attend_local(pairs // 2, pairs)
+    arrive(2)
     last = TILE // PAIR
     early = qw - TILE
 
-    @pl.loop(0, pairs - last)
+    @pl.loop(0, 3)
     def _(g):
-        arrive(g + 1)
-        ready(g)
-        attend(g)
+        attend_remote(g)
+
+    @pl.loop(3, pairs - last)
+    def _(g):
+        arrive(g)
+        attend_remote(g)
 
     for load in loads[6:]:
         load.wait()
@@ -214,11 +246,10 @@
         )
         combined[:, at] = hidden[:, at].astype(jnp.float32) + gate[:, at] * tile
 
-    for g in range(pairs - last, pairs):
-        if g + 1 < pairs:
-            arrive(g + 1)
-        ready(g)
-        attend(g)
+    @pl.loop(pairs - last, pairs)
+    def _(g):
+        arrive(g)
+        attend_remote(g)
 
     for i in range(width // TILE):
         at = pl.ds(i * TILE, TILE)
@@ -234,11 +265,12 @@
         normed[at, :] = layer_norm(combined[at, :]).astype(jnp.bfloat16)
 
     velocity = lax.dot_general(wf[...], normed[...], NT, preferred_element_type=jnp.float32)
-    advanced[...] = latent[...] + step_ref[0] * velocity
-
+    advanced[...] = latent[...] + step[0] * velocity
+
+    keep = pltpu.make_async_copy(advanced, advanced_hbm, load_sem.at[len(loads)])
     seam = pltpu.make_async_remote_copy(
         src_ref=advanced,
-        dst_ref=other,
+        dst_ref=other_hbm,
         send_sem=seam_send,
         recv_sem=seam_recv,
         device_id=partner,
@@ -248,6 +280,8 @@
     @pl.when(has_partner)
     def _():
         seam.start()
+
+    keep.start()
 
     @pl.loop(0, pairs)
     def _(g):
@@ -257,19 +291,11 @@
                 to_peer(j, g, part).wait_send()
                 forward(j, g, part).wait_send()
 
+    keep.wait()
+
     @pl.when(has_partner)
     def _():
-        seam_frames = half_devs * rows
-        first = jnp.where(in_tail, f - half_devs, f) * rows
-        place = first + lax.broadcasted_iota(jnp.int32, advanced.shape, 1)
-        ramp = (place.astype(jnp.float32) + 0.5) / seam_frames
-        own = jnp.where(in_tail, 1.0 - ramp, ramp)
         seam.wait()
-        out_ref[...] = own * advanced[...] + (1.0 - own) * other[...]
-
-    @pl.when(jnp.logical_not(has_partner))
-    def _():
-        out_ref[...] = advanced[...]
 
 
 def on_device(
@@ -293,12 +319,13 @@
     pairs = qw // PAIR
     bf16, f32 = jnp.bfloat16, jnp.float32
     anywhere = pl.BlockSpec(memory_space=pl.ANY)
-    result = pl.pallas_call(
+    advanced, other = pl.pallas_call(
         functools.partial(kernel, windows, frame_devs),
-        out_shape=jax.ShapeDtypeStruct((channels, rows), f32),
-        in_specs=[pl.BlockSpec(memory_space=pltpu.SMEM)] + [anywhere] * 10,
-        out_specs=pl.BlockSpec(memory_space=pltpu.VMEM),
+        out_shape=[jax.ShapeDtypeStruct((channels, rows), f32)] * 2,
+        in_specs=[pl.BlockSpec(memory_space=pltpu.HBM)] + [anywhere] * 10,
+        out_specs=[anywhere] * 2,
         scratch_shapes=[
+            pltpu.SMEM((1,), f32),
             pltpu.VMEM((rows, width), bf16),
             pltpu.VMEM((channels, rows), f32),
             pltpu.VMEM((1, width), f32),
@@ -312,11 +339,13 @@
             pltpu.VMEM((rows, qw), bf16),
             pltpu.VMEM((frame_devs * rows, 2 * qw), bf16),
             pltpu.VMEM((rows, qw), bf16),
+            pltpu.VMEM((rows, qw), f32),
+            pltpu.VMEM((rows, qw), f32),
+            pltpu.VMEM((rows, qw), f32),
             pltpu.VMEM((rows, width), f32),
             pltpu.VMEM((rows, width), bf16),
             pltpu.VMEM((channels, rows), f32),
-            pltpu.VMEM((channels, rows), f32),
-            pltpu.SemaphoreType.DMA((10,)),
+            pltpu.SemaphoreType.DMA((12,)),
             pltpu.SemaphoreType.DMA((frame_devs, pairs, 2)),
             pltpu.SemaphoreType.DMA((frame_devs, pairs, 2)),
             pltpu.SemaphoreType.DMA,
@@ -339,7 +368,16 @@
         w_out,
         w_final.T,
     )
-    return result.T
+    w, f = lax.axis_index("win"), lax.axis_index("frm")
+    half_devs = frame_devs // 2
+    in_tail = f >= half_devs
+    has_partner = jnp.where(in_tail, w < windows - 1, w > 0)
+    first = jnp.where(in_tail, f - half_devs, f) * rows
+    place = first + lax.broadcasted_iota(jnp.int32, (channels, rows), 1)
+    ramp = (place.astype(f32) + 0.5) / (half_devs * rows)
+    own = jnp.where(in_tail, 1.0 - ramp, ramp)
+    blended = jnp.where(has_partner, own * advanced + (1.0 - own) * other, advanced)
+    return blended.T
 
 
 def solution(mesh):

time: 33.8 us -> 33.3 us (0.985)
  other arithmetic: 0 us -> 1.53 us
  local copies, waits for them, and re-layouts: 1.47 us -> 0 us
  Pallas kernels: 31.3 us -> 30.9 us
    transpose x0 -> x1, other arithmetic: none -> 1.52 us  [on_device(): return blended.T]
    unnamed x1 -> x0, local copies, waits for them, and re-layouts: 1.47 us -> none
    pallas_call x1, Pallas kernels: 31.3 us -> 30.9 us  [on_device(): pl.pallas_call(functools.partial(kernel, windows, frame_devs), out_shape=...]
where the time goes in v2:
time: 33.3 us; the launch traced here: 33.1 us
  Pallas kernels  30.9 us (93%)
  other arithmetic  1.53 us (5%)
  between operations  0.67 us (2%)
    pallas_call x1, Pallas kernels, on_device(): pl.pallas_call(functools.partial(kernel, windows, frame_devs), out_shape=...  30.9 us
    transpose x1, other arithmetic, on_device(): return blended.T  1.52 us

profile of v2, /device:TPU:21, one launch (start us, length us, event | category | flops | bytes accessed | tf_op | source)
XLA Modules:
  0.0 33.1 jit_solution(6629454811419985403)
XLA Ops:
  0.7 30.9 %dit_window_step.1 = (f32[64,256]{1,0:T(8,128)}, f32[64,256]{1,0:T(8,128)}) custom-call(f32[1]{0:T(128)S(6)} %copy.12.step_hbm, bf16[256,1536]{1,0:T(8,128)(2,1)} %hidden_hbm.1, f32[64,256]{1,0:T(8,128)} %bitcast.5, bf16[256,1536]{1,0:T(8,128)(2,1)} %stale_hbm.1, f32[1,1536]{1,0:T(1,128)} %shift_hbm.1, f32[1,1536]{1,0:T(1,128)} %scale_hbm.1, ...), custom_call_target="tpu_custom_call" | custom-call | tf_op jit(solution)/shard_map/dit_window_step/pallas_call | solution.py:322
  31.6 1.5 %select_bitcast_fusion = f32[256,64]{0,1:T(8,128)} fusion(f32[64,256]{1,0:T(8,128)} %get-tuple-element.7, f32[64,256]{1,0:T(8,128)} %get-tuple-element.8, f32[256]{0:T(256)S(1)} %get-tuple-element.10, f32[256]{0:T(256)S(1)} %get-tuple-element.9, pred[]{:T(512)S(6)} %select_n.23), kind=kLoop, calls=%fused_computation | loop fusion | flops 65536 | bytes 198657 | tf_op jit(solution)/shard_map/transpose | solution.py:380
  (1 shorter events, 0.0 us)

commit v3 on v2

--- a/solution.py
+++ b/solution.py
@@ -8,6 +8,7 @@
 from jax.sharding import PartitionSpec as P
 
 HEAD_DIM = 64
+AHEAD = 3
 PAIR = 2 * HEAD_DIM
 TILE = 256
 LN_ROWS = 32
@@ -50,6 +51,7 @@
     wf,
     modulated,
     queries,
+    own,
     kv,
     attention,
     maxima,
@@ -59,6 +61,7 @@
     normed,
     advanced,
     load_sem,
+    stage_sem,
     send_sem,
     recv_sem,
     seam_send,
@@ -99,6 +102,17 @@
             ]
         )
     ]
+    def stage(g, part):
+        at = pl.ds(pl.multiple_of(part * qw + g * PAIR, PAIR), PAIR)
+        return pltpu.make_async_copy(
+            stale_hbm.at[:, at], own.at[part * pairs + g], stage_sem.at[g, part]
+        )
+
+    @pl.loop(0, pairs)
+    def _(g):
+        for part in range(2):
+            stage(g, part).start()
+
     for load in loads:
         load.start()
 
@@ -112,13 +126,13 @@
 
     pl.semaphore_wait(barrier, jnp.where(has_partner, chips + 1, chips))
 
-    def columns(g, part):
-        return pl.ds(pl.multiple_of(part * qw + g * PAIR, PAIR), PAIR)
+    def columns(g):
+        return pl.ds(pl.multiple_of(g * PAIR, PAIR), PAIR)
 
     def send(source, slot, device, g, part):
         return pltpu.make_async_remote_copy(
-            src_ref=source.at[:, columns(g, part)],
-            dst_ref=kv.at[pl.ds(slot * rows, rows), columns(g, part)],
+            src_ref=source,
+            dst_ref=kv.at[part * pairs + g, pl.ds(slot * rows, rows)],
             send_sem=send_sem.at[slot, g, part],
             recv_sem=recv_sem.at[slot, g, part],
             device_id=device,
@@ -126,20 +140,19 @@
         )
 
     def to_sibling(g, part):
-        return send(stale_hbm, 1, sibling, g, part)
+        return send(own.at[part * pairs + g], 1, sibling, g, part)
 
     def to_peer(j, g, part):
-        return send(stale_hbm, 2 * j, peers[j - 1], g, part)
+        return send(own.at[part * pairs + g], 2 * j, peers[j - 1], g, part)
 
     def forward(j, g, part):
-        return send(kv.at[pl.ds(2 * j * rows, rows)], 2 * j + 1, sibling, g, part)
-
-    @pl.loop(0, pairs)
-    def _(g):
+        source = kv.at[part * pairs + g, pl.ds(2 * j * rows, rows)]
+        return send(source, 2 * j + 1, sibling, g, part)
+
+    def launch(g):
         for part in range(2):
             for j in range(1, chips):
                 to_peer(j, g, part).start()
-            to_sibling(g, part).start()
 
     def arrive(g):
         for j in range(1, chips):
@@ -147,6 +160,33 @@
                 to_peer(j, g, part).wait_recv()
                 forward(j, g, part).start()
 
+    @pl.loop(0, AHEAD)
+    def _(g):
+        for part in range(2):
+            stage(g, part).wait()
+        launch(g)
+        for part in range(2):
+            to_sibling(g, part).start()
+
+    def advance(g):
+        arrive(g)
+        for part in range(2):
+            for j in range(1, chips):
+                to_peer(j, g, part).wait_send()
+        if isinstance(g, int):
+            if g + AHEAD < pairs:
+                launch(g + AHEAD)
+        else:
+            @pl.when(g + AHEAD < pairs)
+            def _():
+                launch(g + AHEAD)
+
+    @pl.loop(AHEAD, pairs)
+    def _(g):
+        for part in range(2):
+            stage(g, part).wait()
+            to_sibling(g, part).start()
+
     for load in loads[:3]:
         load.wait()
 
@@ -171,15 +211,17 @@
     def _(i):
         at = pl.ds(pl.multiple_of(i * TILE, TILE), TILE)
         tile = jnp.dot(modulated[...], wkv[:, at], preferred_element_type=jnp.float32)
-        kv[pl.ds(0, rows), at] = tile.astype(jnp.bfloat16)
+        for k in range(TILE // PAIR):
+            piece = tile[:, k * PAIR : (k + 1) * PAIR].astype(jnp.bfloat16)
+            kv[(TILE // PAIR) * i + k, pl.ds(0, rows)] = piece
 
     low = lax.broadcasted_iota(jnp.int32, (rows, PAIR), 1) < HEAD_DIM
 
     def attend(g, slot, slots, first, final):
-        at = columns(g, 0)
+        at = columns(g)
         held = pl.ds(slot * rows, slots * rows)
         query = queries[:, at].astype(jnp.float32)
-        keys, values = kv[held, at], kv[held, columns(g, 1)]
+        keys, values = kv[g, held], kv[pairs + g, held]
         heads = []
         for chosen in (low, jnp.logical_not(low)):
             masked = jnp.where(chosen, query, 0.0).astype(jnp.bfloat16)
@@ -217,11 +259,11 @@
                 forward(j, g, part).wait_recv()
             attend(g, 2 * j + 1, 1, False, j == chips - 1)
 
-    arrive(0)
+    advance(0)
     attend_local(0, pairs // 2)
-    arrive(1)
+    advance(1)
     attend_local(pairs // 2, pairs)
-    arrive(2)
+    advance(2)
     last = TILE // PAIR
     early = qw - TILE
 
@@ -231,7 +273,7 @@
 
     @pl.loop(3, pairs - last)
     def _(g):
-        arrive(g)
+        advance(g)
         attend_remote(g)
 
     for load in loads[6:]:
@@ -248,7 +290,7 @@
 
     @pl.loop(pairs - last, pairs)
     def _(g):
-        arrive(g)
+        advance(g)
         attend_remote(g)
 
     for i in range(width // TILE):
@@ -288,7 +330,6 @@
         for part in range(2):
             to_sibling(g, part).wait_send()
             for j in range(1, chips):
-                to_peer(j, g, part).wait_send()
                 forward(j, g, part).wait_send()
 
     keep.wait()
@@ -322,7 +363,7 @@
     advanced, other = pl.pallas_call(
         functools.partial(kernel, windows, frame_devs),
         out_shape=[jax.ShapeDtypeStruct((channels, rows), f32)] * 2,
-        in_specs=[pl.BlockSpec(memory_space=pltpu.HBM)] + [anywhere] * 10,
+        in_specs=[anywhere] + [pl.BlockSpec(memory_space=pltpu.HBM)] * 10,
         out_specs=[anywhere] * 2,
         scratch_shapes=[
             pltpu.SMEM((1,), f32),
@@ -337,7 +378,8 @@
             pltpu.VMEM((channels, width), bf16),
             pltpu.VMEM((rows, width), bf16),
             pltpu.VMEM((rows, qw), bf16),
-            pltpu.VMEM((frame_devs * rows, 2 * qw), bf16),
+            pltpu.VMEM((2 * pairs, rows, PAIR), bf16),
+            pltpu.VMEM((2 * pairs, frame_devs * rows, PAIR), bf16),
             pltpu.VMEM((rows, qw), bf16),
             pltpu.VMEM((rows, qw), f32),
             pltpu.VMEM((rows, qw), f32),
@@ -346,27 +388,33 @@
             pltpu.VMEM((rows, width), bf16),
             pltpu.VMEM((channels, rows), f32),
             pltpu.SemaphoreType.DMA((12,)),
+            pltpu.SemaphoreType.DMA((pairs, 2)),
             pltpu.SemaphoreType.DMA((frame_devs, pairs, 2)),
             pltpu.SemaphoreType.DMA((frame_devs, pairs, 2)),
             pltpu.SemaphoreType.DMA,
             pltpu.SemaphoreType.DMA,
         ],
         compiler_params=pltpu.CompilerParams(
-            collective_id=0, has_side_effects=True, vmem_limit_bytes=56 * 1024 * 1024
+            collective_id=0, has_side_effects=True, vmem_limit_bytes=44 * 1024 * 1024
         ),
         name="dit_window_step",
     )(
         step_size,
-        hidden_state,
-        latent.T,
-        stale_kv,
-        mod_shift,
-        mod_scale,
-        mod_gate,
-        w_query,
-        w_keyval,
-        w_out,
-        w_final.T,
+        *(
+            pltpu.with_memory_space_constraint(operand, pltpu.HBM)
+            for operand in (
+                hidden_state,
+                latent.T,
+                stale_kv,
+                mod_shift,
+                mod_scale,
+                mod_gate,
+                w_query,
+                w_keyval,
+                w_out,
+                w_final.T,
+            )
+        )
     )
     w, f = lax.axis_index("win"), lax.axis_index("frm")
     half_devs = frame_devs // 2

time: 33.3 us -> 32.2 us (0.967)
  other arithmetic: 1.53 us -> 0.66 us
    transpose x1, other arithmetic: 1.52 us -> 0.65 us  [on_device(): return blended.T]
where the time goes in v3:
time: 32.2 us; the launch traced here: 32.1 us
  Pallas kernels  30.8 us (96%)
  between operations  0.67 us (2%)
  other arithmetic  0.66 us (2%)
    pallas_call x1, Pallas kernels, on_device(): pl.pallas_call(functools.partial(kernel, windows, frame_devs), out_shape=...  30.8 us
    transpose x1, other arithmetic, on_device(): return blended.T  0.65 us

profile of v3, /device:TPU:21, one launch (start us, length us, event | category | flops | bytes accessed | tf_op | source)
XLA Modules:
  0.0 32.1 jit_solution(6110935962595359943)
XLA Ops:
  0.7 30.8 %dit_window_step.1 = (f32[64,256]{1,0:T(8,128)S(1)}, f32[64,256]{1,0:T(8,128)S(1)}) custom-call(f32[1]{0:T(128)S(6)} %copy.12.step_hbm, bf16[256,1536]{1,0:T(8,128)(2,1)} %hidden_hbm.1, f32[64,256]{1,0:T(8,128)} %bitcast.5, bf16[256,1536]{1,0:T(8,128)(2,1)} %stale_hbm.1, f32[1,1536]{1,0:T(1,128)} %shift_hbm.1, f32[1,1536]{1,0:T(1,128)} %scale_hbm.1, ...), custom_call_target="tpu_custom_call" | custom-call | tf_op jit(solution)/shard_map/dit_window_step/pallas_call | solution.py:363
  31.4 0.6 %select_bitcast_fusion = f32[256,64]{0,1:T(8,128)} fusion(f32[64,256]{1,0:T(8,128)S(1)} %get-tuple-element.7, f32[64,256]{1,0:T(8,128)S(1)} %get-tuple-element.8, f32[256]{0:T(256)S(1)} %get-tuple-element.10, f32[256]{0:T(256)S(1)} %get-tuple-element.9, pred[]{:T(512)S(6)} %select_n.23), kind=kLoop, calls=%fused_computation | loop fusion | flops 65536 | bytes 198657 | tf_op jit(solution)/shard_map/transpose | solution.py:428
  (1 shorter events, 0.0 us)

commit v4 on v3

--- a/solution.py
+++ b/solution.py
@@ -11,9 +11,8 @@
 AHEAD = 3
 PAIR = 2 * HEAD_DIM
 TILE = 256
-LN_ROWS = 32
+LN_ROWS = 64
 MESH = pl.DeviceIdType.MESH
-NT = (((1,), (1,)), ((), ()))
 
 
 def layer_norm(values):
@@ -21,6 +20,10 @@
     centred = values - average
     variance = jnp.mean(centred * centred, axis=-1, keepdims=True)
     return centred * lax.rsqrt(variance + 1e-06)
+
+
+def flip(block):
+    return block.astype(jnp.float32).T.astype(block.dtype)
 
 
 def kernel(
@@ -49,10 +52,13 @@
     wkv,
     wo,
     wf,
+    wf_rows,
     modulated,
     queries,
+    staged,
     own,
-    kv,
+    keys,
+    values,
     attention,
     maxima,
     totals,
@@ -68,7 +74,7 @@
     seam_recv,
 ):
     rows, width = hidden.shape
-    qw = queries.shape[1]
+    qw = wq.shape[1]
     pairs = qw // PAIR
     chips = frame_devs // 2
     half_devs = frame_devs // 2
@@ -105,7 +111,7 @@
     def stage(g, part):
         at = pl.ds(pl.multiple_of(part * qw + g * PAIR, PAIR), PAIR)
         return pltpu.make_async_copy(
-            stale_hbm.at[:, at], own.at[part * pairs + g], stage_sem.at[g, part]
+            stale_hbm.at[:, at], staged.at[part * pairs + g], stage_sem.at[g, part]
         )
 
     @pl.loop(0, pairs)
@@ -129,10 +135,16 @@
     def columns(g):
         return pl.ds(pl.multiple_of(g * PAIR, PAIR), PAIR)
 
-    def send(source, slot, device, g, part):
+    def place(slot, g, part):
+        return values.at[g, slot] if part else keys.at[g, pl.ds(slot * rows, rows)]
+
+    def source(g, part):
+        return own.at[g] if part else staged.at[g]
+
+    def send(ref, slot, device, g, part):
         return pltpu.make_async_remote_copy(
-            src_ref=source,
-            dst_ref=kv.at[part * pairs + g, pl.ds(slot * rows, rows)],
+            src_ref=ref,
+            dst_ref=place(slot, g, part),
             send_sem=send_sem.at[slot, g, part],
             recv_sem=recv_sem.at[slot, g, part],
             device_id=device,
@@ -140,19 +152,17 @@
         )
 
     def to_sibling(g, part):
-        return send(own.at[part * pairs + g], 1, sibling, g, part)
+        return send(source(g, part), 1, sibling, g, part)
 
     def to_peer(j, g, part):
-        return send(own.at[part * pairs + g], 2 * j, peers[j - 1], g, part)
+        return send(source(g, part), 2 * j, peers[j - 1], g, part)
 
     def forward(j, g, part):
-        source = kv.at[part * pairs + g, pl.ds(2 * j * rows, rows)]
-        return send(source, 2 * j + 1, sibling, g, part)
-
-    def launch(g):
-        for part in range(2):
-            for j in range(1, chips):
-                to_peer(j, g, part).start()
+        return send(place(2 * j, g, part), 2 * j + 1, sibling, g, part)
+
+    def launch(g, part):
+        for j in range(1, chips):
+            to_peer(j, g, part).start()
 
     def arrive(g):
         for j in range(1, chips):
@@ -160,12 +170,17 @@
                 to_peer(j, g, part).wait_recv()
                 forward(j, g, part).start()
 
-    @pl.loop(0, AHEAD)
+    @pl.loop(0, pairs)
     def _(g):
         for part in range(2):
             stage(g, part).wait()
-        launch(g)
-        for part in range(2):
+            if part:
+                own[g] = flip(staged[pairs + g])
+
+            @pl.when(g < AHEAD)
+            def _():
+                launch(g, part)
+
             to_sibling(g, part).start()
 
     def advance(g):
@@ -173,77 +188,87 @@
         for part in range(2):
             for j in range(1, chips):
                 to_peer(j, g, part).wait_send()
-        if isinstance(g, int):
-            if g + AHEAD < pairs:
-                launch(g + AHEAD)
-        else:
-            @pl.when(g + AHEAD < pairs)
-            def _():
-                launch(g + AHEAD)
-
-    @pl.loop(AHEAD, pairs)
-    def _(g):
-        for part in range(2):
-            stage(g, part).wait()
-            to_sibling(g, part).start()
+
+        @pl.when(g + AHEAD < pairs)
+        def _():
+            for part in range(2):
+                launch(g + AHEAD, part)
 
     for load in loads[:3]:
         load.wait()
 
-    @pl.loop(0, rows // LN_ROWS)
-    def _(i):
-        at = pl.ds(pl.multiple_of(i * LN_ROWS, LN_ROWS), LN_ROWS)
+    for start in range(0, rows, LN_ROWS):
+        at = pl.ds(start, LN_ROWS)
         line = layer_norm(hidden[at, :].astype(jnp.float32))
         modulated[at, :] = (line * (1.0 + scale[...]) + shift[...]).astype(jnp.bfloat16)
 
     loads[3].wait()
+    blank = jnp.zeros((HEAD_DIM, rows), jnp.bfloat16)
 
     @pl.loop(0, qw // TILE)
     def _(i):
         at = pl.ds(pl.multiple_of(i * TILE, TILE), TILE)
         tile = jnp.dot(modulated[...], wq[:, at], preferred_element_type=jnp.float32)
-        queries[:, at] = (tile * HEAD_DIM ** (-0.5)).astype(jnp.bfloat16)
+        tile = (tile * HEAD_DIM ** (-0.5)).T.astype(jnp.bfloat16)
+        for k in range(TILE // PAIR):
+            g = (TILE // PAIR) * i + k
+            first, second = k * PAIR, k * PAIR + HEAD_DIM
+            queries[g, 0:HEAD_DIM, 0:rows] = tile[first:second]
+            queries[g, HEAD_DIM:PAIR, 0:rows] = blank
+            queries[g, 0:HEAD_DIM, rows : 2 * rows] = blank
+            queries[g, HEAD_DIM:PAIR, rows : 2 * rows] = tile[second : second + HEAD_DIM]
 
     loads[4].wait()
-    loads[5].wait()
-
-    @pl.loop(0, 2 * qw // TILE)
+
+    @pl.loop(0, qw // TILE)
     def _(i):
         at = pl.ds(pl.multiple_of(i * TILE, TILE), TILE)
         tile = jnp.dot(modulated[...], wkv[:, at], preferred_element_type=jnp.float32)
         for k in range(TILE // PAIR):
             piece = tile[:, k * PAIR : (k + 1) * PAIR].astype(jnp.bfloat16)
-            kv[(TILE // PAIR) * i + k, pl.ds(0, rows)] = piece
-
-    low = lax.broadcasted_iota(jnp.int32, (rows, PAIR), 1) < HEAD_DIM
+            keys[(TILE // PAIR) * i + k, 0:rows] = piece
+
+    loads[5].wait()
+
+    @pl.loop(0, qw // TILE)
+    def _(i):
+        at = pl.ds(pl.multiple_of(qw + i * TILE, TILE), TILE)
+        tile = jnp.dot(modulated[...], wkv[:, at], preferred_element_type=jnp.float32)
+        tile = tile.T.astype(jnp.bfloat16)
+        for k in range(TILE // PAIR):
+            values[(TILE // PAIR) * i + k, 0] = tile[k * PAIR : (k + 1) * PAIR]
 
     def attend(g, slot, slots, first, final):
-        at = columns(g)
-        held = pl.ds(slot * rows, slots * rows)
-        query = queries[:, at].astype(jnp.float32)
-        keys, values = kv[g, held], kv[pairs + g, held]
+        scores = jnp.dot(
+            keys[g, pl.ds(slot * rows, slots * rows)], queries[g],
+            preferred_element_type=jnp.float32,
+        )
+        top = jnp.max(scores, axis=0, keepdims=True)
+        if not first:
+            top = jnp.maximum(maxima[g], top)
+        probs = jnp.exp(scores - top)
+        total = jnp.sum(probs, axis=0, keepdims=True)
+        if not first:
+            kept = jnp.exp(maxima[g] - top)
+            total = totals[g] * kept + total
+        weights = probs.astype(jnp.bfloat16)
         heads = []
-        for chosen in (low, jnp.logical_not(low)):
-            masked = jnp.where(chosen, query, 0.0).astype(jnp.bfloat16)
-            scores = lax.dot_general(masked, keys, NT, preferred_element_type=jnp.float32)
-            top = jnp.max(scores, axis=-1, keepdims=True)
-            probs = jnp.exp(scores - top)
-            total = jnp.sum(probs, axis=-1, keepdims=True)
-            summed = jnp.dot(
-                probs.astype(jnp.bfloat16), values, preferred_element_type=jnp.float32
-            )
-            heads.append((top, total, summed))
-        top, total, summed = (jnp.where(low, *both) for both in zip(*heads))
-        if not first:
-            peak = jnp.maximum(maxima[:, at], top)
-            keep, add = jnp.exp(maxima[:, at] - peak), jnp.exp(top - peak)
-            top = peak
-            total = totals[:, at] * keep + total * add
-            summed = running[:, at] * keep + summed * add
+        for head in range(2):
+            lanes = slice(head * rows, (head + 1) * rows)
+            span = slice(head * HEAD_DIM, (head + 1) * HEAD_DIM)
+            summed = running[g, span] * kept[:, lanes] if not first else None
+            for k in range(slots):
+                share = jnp.dot(
+                    values[g, slot + k, span], weights[k * rows : (k + 1) * rows, lanes],
+                    preferred_element_type=jnp.float32,
+                )
+                summed = share if summed is None else summed + share
+            heads.append(summed / total[:, lanes] if final else summed)
+        both = jnp.concatenate(heads, axis=0)
         if final:
-            attention[:, at] = (summed / total).astype(jnp.bfloat16)
+            attention[:, columns(g)] = both.T.astype(jnp.bfloat16)
         else:
-            maxima[:, at], totals[:, at], running[:, at] = top, total, summed
+            maxima[g], totals[g], running[g] = top, total, both
 
     def attend_local(start, stop):
         @pl.loop(start, stop)
@@ -252,12 +277,16 @@
                 to_sibling(g, part).wait_recv()
             attend(g, 0, 2, True, chips == 1)
 
-    def attend_remote(g):
+    def attend_remote(g, together):
         for j in range(1, chips):
-            attend(g, 2 * j, 1, False, False)
+            if not together:
+                attend(g, 2 * j, 1, False, False)
             for part in range(2):
                 forward(j, g, part).wait_recv()
-            attend(g, 2 * j + 1, 1, False, j == chips - 1)
+            if together:
+                attend(g, 2 * j, 2, False, j == chips - 1)
+            else:
+                attend(g, 2 * j + 1, 1, False, j == chips - 1)
 
     advance(0)
     attend_local(0, pairs // 2)
@@ -269,15 +298,16 @@
 
     @pl.loop(0, 3)
     def _(g):
-        attend_remote(g)
+        attend_remote(g, True)
 
     @pl.loop(3, pairs - last)
     def _(g):
         advance(g)
-        attend_remote(g)
+        attend_remote(g, False)
 
     for load in loads[6:]:
         load.wait()
+    wf_rows[...] = flip(wf[...])
 
     @pl.loop(0, width // TILE)
     def _(i):
@@ -291,7 +321,7 @@
     @pl.loop(pairs - last, pairs)
     def _(g):
         advance(g)
-        attend_remote(g)
+        attend_remote(g, False)
 
     for i in range(width // TILE):
         at = pl.ds(i * TILE, TILE)
@@ -301,13 +331,12 @@
         )
         combined[:, at] += gate[:, at] * tile
 
-    @pl.loop(0, rows // LN_ROWS)
-    def _(i):
-        at = pl.ds(pl.multiple_of(i * LN_ROWS, LN_ROWS), LN_ROWS)
+    for start in range(0, rows, LN_ROWS):
+        at = pl.ds(start, LN_ROWS)
         normed[at, :] = layer_norm(combined[at, :]).astype(jnp.bfloat16)
 
-    velocity = lax.dot_general(wf[...], normed[...], NT, preferred_element_type=jnp.float32)
-    advanced[...] = latent[...] + step[0] * velocity
+    velocity = jnp.dot(normed[...], wf_rows[...], preferred_element_type=jnp.float32)
+    advanced[...] = latent[...] + step[0] * velocity.T
 
     keep = pltpu.make_async_copy(advanced, advanced_hbm, load_sem.at[len(loads)])
     seam = pltpu.make_async_remote_copy(
@@ -376,14 +405,17 @@
             pltpu.VMEM(w_keyval.shape, bf16),
             pltpu.VMEM(w_out.shape, bf16),
             pltpu.VMEM((channels, width), bf16),
+            pltpu.VMEM((width, channels), bf16),
             pltpu.VMEM((rows, width), bf16),
+            pltpu.VMEM((pairs, PAIR, 2 * rows), bf16),
+            pltpu.VMEM((2 * pairs, rows, PAIR), bf16),
+            pltpu.VMEM((pairs, PAIR, rows), bf16),
+            pltpu.VMEM((pairs, frame_devs * rows, PAIR), bf16),
+            pltpu.VMEM((pairs, frame_devs, PAIR, rows), bf16),
             pltpu.VMEM((rows, qw), bf16),
-            pltpu.VMEM((2 * pairs, rows, PAIR), bf16),
-            pltpu.VMEM((2 * pairs, frame_devs * rows, PAIR), bf16),
-            pltpu.VMEM((rows, qw), bf16),
-            pltpu.VMEM((rows, qw), f32),
-            pltpu.VMEM((rows, qw), f32),
-            pltpu.VMEM((rows, qw), f32),
+            pltpu.VMEM((pairs, 1, 2 * rows), f32),
+            pltpu.VMEM((pairs, 1, 2 * rows), f32),
+            pltpu.VMEM((pairs, PAIR, rows), f32),
             pltpu.VMEM((rows, width), f32),
             pltpu.VMEM((rows, width), bf16),
             pltpu.VMEM((channels, rows), f32),

time: 32.2 us -> 30.2 us (0.938)
  Pallas kernels: 30.8 us -> 28.7 us
    pallas_call x1, Pallas kernels: 30.8 us -> 28.7 us  [on_device(): pl.pallas_call(functools.partial(kernel, windows, frame_devs), out_shape=...]
where the time goes in v4:
time: 30.2 us; the launch traced here: 30 us
  Pallas kernels  28.7 us (95%)
  between operations  0.67 us (2%)
  other arithmetic  0.66 us (2%)
    pallas_call x1, Pallas kernels, on_device(): pl.pallas_call(functools.partial(kernel, windows, frame_devs), out_shape=...  28.7 us
    transpose x1, other arithmetic, on_device(): return blended.T  0.65 us

profile of v4, /device:TPU:21, one launch (start us, length us, event | category | flops | bytes accessed | tf_op | source)
XLA Modules:
  0.0 30.0 jit_solution(15974468623445511460)
XLA Ops:
  0.7 28.7 %dit_window_step.1 = (f32[64,256]{1,0:T(8,128)S(1)}, f32[64,256]{1,0:T(8,128)S(1)}) custom-call(f32[1]{0:T(128)S(6)} %copy.12.step_hbm, bf16[256,1536]{1,0:T(8,128)(2,1)} %hidden_hbm.1, f32[64,256]{1,0:T(8,128)} %bitcast.5, bf16[256,1536]{1,0:T(8,128)(2,1)} %stale_hbm.1, f32[1,1536]{1,0:T(1,128)} %shift_hbm.1, f32[1,1536]{1,0:T(1,128)} %scale_hbm.1, ...), custom_call_target="tpu_custom_call" | custom-call | tf_op jit(solution)/shard_map/dit_window_step/pallas_call | solution.py:392
  29.4 0.6 %select_bitcast_fusion = f32[256,64]{0,1:T(8,128)} fusion(f32[64,256]{1,0:T(8,128)S(1)} %get-tuple-element.7, f32[64,256]{1,0:T(8,128)S(1)} %get-tuple-element.8, f32[256]{0:T(256)S(1)} %get-tuple-element.10, f32[256]{0:T(256)S(1)} %get-tuple-element.9, pred[]{:T(512)S(6)} %select_n.23), kind=kLoop, calls=%fused_computation | loop fusion | flops 65536 | bytes 198657 | tf_op jit(solution)/shard_map/transpose | solution.py:460
  (1 shorter events, 0.0 us)

commit v5 on v4

--- a/solution.py
+++ b/solution.py
@@ -8,7 +8,7 @@
 from jax.sharding import PartitionSpec as P
 
 HEAD_DIM = 64
-AHEAD = 3
+AHEAD = 4
 PAIR = 2 * HEAD_DIM
 TILE = 256
 LN_ROWS = 64
@@ -66,6 +66,7 @@
     combined,
     normed,
     advanced,
+    sent,
     load_sem,
     stage_sem,
     send_sem,
@@ -331,27 +332,33 @@
         )
         combined[:, at] += gate[:, at] * tile
 
-    for start in range(0, rows, LN_ROWS):
-        at = pl.ds(start, LN_ROWS)
-        normed[at, :] = layer_norm(combined[at, :]).astype(jnp.bfloat16)
-
-    velocity = jnp.dot(normed[...], wf_rows[...], preferred_element_type=jnp.float32)
-    advanced[...] = latent[...] + step[0] * velocity.T
+    def seam(half):
+        at = pl.ds(half * (rows // 2), rows // 2)
+        return pltpu.make_async_remote_copy(
+            src_ref=sent.at[:, at],
+            dst_ref=other_hbm.at[:, at],
+            send_sem=seam_send.at[half],
+            recv_sem=seam_recv.at[half],
+            device_id=partner,
+            device_id_type=MESH,
+        )
+
+    for half in range(2):
+        first = half * (rows // 2)
+        for start in range(first, first + rows // 2, LN_ROWS):
+            at = pl.ds(start, LN_ROWS)
+            normed[at, :] = layer_norm(combined[at, :]).astype(jnp.bfloat16)
+        at = pl.ds(first, rows // 2)
+        velocity = jnp.dot(normed[at, :], wf_rows[...], preferred_element_type=jnp.float32)
+        moved = latent[:, at] + step[0] * velocity.T
+        advanced[:, at] = moved
+        sent[:, at] = moved.astype(jnp.bfloat16)
+
+        @pl.when(has_partner)
+        def _():
+            seam(half).start()
 
     keep = pltpu.make_async_copy(advanced, advanced_hbm, load_sem.at[len(loads)])
-    seam = pltpu.make_async_remote_copy(
-        src_ref=advanced,
-        dst_ref=other_hbm,
-        send_sem=seam_send,
-        recv_sem=seam_recv,
-        device_id=partner,
-        device_id_type=MESH,
-    )
-
-    @pl.when(has_partner)
-    def _():
-        seam.start()
-
     keep.start()
 
     @pl.loop(0, pairs)
@@ -365,7 +372,8 @@
 
     @pl.when(has_partner)
     def _():
-        seam.wait()
+        for half in range(2):
+            seam(half).wait()
 
 
 def on_device(
@@ -391,7 +399,7 @@
     anywhere = pl.BlockSpec(memory_space=pl.ANY)
     advanced, other = pl.pallas_call(
         functools.partial(kernel, windows, frame_devs),
-        out_shape=[jax.ShapeDtypeStruct((channels, rows), f32)] * 2,
+        out_shape=[jax.ShapeDtypeStruct((channels, rows), dtype) for dtype in (f32, bf16)],
         in_specs=[anywhere] + [pl.BlockSpec(memory_space=pltpu.HBM)] * 10,
         out_specs=[anywhere] * 2,
         scratch_shapes=[
@@ -419,12 +427,13 @@
             pltpu.VMEM((rows, width), f32),
             pltpu.VMEM((rows, width), bf16),
             pltpu.VMEM((channels, rows), f32),
+            pltpu.VMEM((channels, rows), bf16),
             pltpu.SemaphoreType.DMA((12,)),
             pltpu.SemaphoreType.DMA((pairs, 2)),
             pltpu.SemaphoreType.DMA((frame_devs, pairs, 2)),
             pltpu.SemaphoreType.DMA((frame_devs, pairs, 2)),
-            pltpu.SemaphoreType.DMA,
-            pltpu.SemaphoreType.DMA,
+            pltpu.SemaphoreType.DMA((2,)),
+            pltpu.SemaphoreType.DMA((2,)),
         ],
         compiler_params=pltpu.CompilerParams(
             collective_id=0, has_side_effects=True, vmem_limit_bytes=44 * 1024 * 1024

time: 30.2 us -> 29.5 us (0.977)
  Pallas kernels: 28.7 us -> 28 us
    pallas_call x1, Pallas kernels: 28.7 us -> 28 us  [on_device(): pl.pallas_call(functools.partial(kernel, windows, frame_devs), out_shape=...]
where the time goes in v5:
time: 29.5 us; the launch traced here: 29.3 us
  Pallas kernels  28 us (95%)
  between operations  0.67 us (2%)
  other arithmetic  0.66 us (2%)
    pallas_call x1, Pallas kernels, on_device(): pl.pallas_call(functools.partial(kernel, windows, frame_devs), out_shape=...  28 us
    transpose x1, other arithmetic, on_device(): return blended.T  0.65 us

profile of v5, /device:TPU:21, one launch (start us, length us, event | category | flops | bytes accessed | tf_op | source)
XLA Modules:
  0.0 29.3 jit_solution(4073790451396882245)
XLA Ops:
  0.7 28.0 %dit_window_step.1 = (f32[64,256]{1,0:T(8,128)S(1)}, bf16[64,256]{1,0:T(8,128)(2,1)S(1)}) custom-call(f32[1]{0:T(128)S(6)} %copy.12.step_hbm, bf16[256,1536]{1,0:T(8,128)(2,1)} %hidden_hbm.1, f32[64,256]{1,0:T(8,128)} %bitcast.5, bf16[256,1536]{1,0:T(8,128)(2,1)} %stale_hbm.1, f32[1,1536]{1,0:T(1,128)} %shift_hbm.1, f32[1,1536]{1,0:T(1,128)} %scale_hbm.1, ...), custom_call_target="tpu_custom_call" | custom-call | tf_op jit(solution)/shard_map/dit_window_step/pallas_call | solution.py:400
  28.7 0.6 %select_bitcast_fusion = f32[256,64]{0,1:T(8,128)} fusion(f32[64,256]{1,0:T(8,128)S(1)} %get-tuple-element.7, bf16[64,256]{1,0:T(8,128)(2,1)S(1)} %get-tuple-element.8, f32[256]{0:T(256)S(1)} %get-tuple-element.10, f32[256]{0:T(256)S(1)} %get-tuple-element.9, pred[]{:T(512)S(6)} %select_n.23), kind=kLoop, calls=%fused_computation | loop fusion | flops 81920 | bytes 165889 | tf_op jit(solution)/shard_map/transpose | solution.py:469
  (1 shorter events, 0.0 us)

commit v6 on v5

--- a/solution.py
+++ b/solution.py
@@ -134,7 +134,7 @@
     pl.semaphore_wait(barrier, jnp.where(has_partner, chips + 1, chips))
 
     def columns(g):
-        return pl.ds(pl.multiple_of(g * PAIR, PAIR), PAIR)
+        return pl.ds(g * PAIR, PAIR)
 
     def place(slot, g, part):
         return values.at[g, slot] if part else keys.at[g, pl.ds(slot * rows, rows)]
@@ -186,12 +186,7 @@
 
     def advance(g):
         arrive(g)
-        for part in range(2):
-            for j in range(1, chips):
-                to_peer(j, g, part).wait_send()
-
-        @pl.when(g + AHEAD < pairs)
-        def _():
+        if g + AHEAD < pairs:
             for part in range(2):
                 launch(g + AHEAD, part)
 
@@ -206,9 +201,8 @@
     loads[3].wait()
     blank = jnp.zeros((HEAD_DIM, rows), jnp.bfloat16)
 
-    @pl.loop(0, qw // TILE)
-    def _(i):
-        at = pl.ds(pl.multiple_of(i * TILE, TILE), TILE)
+    for i in range(qw // TILE):
+        at = pl.ds(i * TILE, TILE)
         tile = jnp.dot(modulated[...], wq[:, at], preferred_element_type=jnp.float32)
         tile = (tile * HEAD_DIM ** (-0.5)).T.astype(jnp.bfloat16)
         for k in range(TILE // PAIR):
@@ -221,9 +215,8 @@
 
     loads[4].wait()
 
-    @pl.loop(0, qw // TILE)
-    def _(i):
-        at = pl.ds(pl.multiple_of(i * TILE, TILE), TILE)
+    for i in range(qw // TILE):
+        at = pl.ds(i * TILE, TILE)
         tile = jnp.dot(modulated[...], wkv[:, at], preferred_element_type=jnp.float32)
         for k in range(TILE // PAIR):
             piece = tile[:, k * PAIR : (k + 1) * PAIR].astype(jnp.bfloat16)
@@ -231,9 +224,8 @@
 
     loads[5].wait()
 
-    @pl.loop(0, qw // TILE)
-    def _(i):
-        at = pl.ds(pl.multiple_of(qw + i * TILE, TILE), TILE)
+    for i in range(qw // TILE):
+        at = pl.ds(qw + i * TILE, TILE)
         tile = jnp.dot(modulated[...], wkv[:, at], preferred_element_type=jnp.float32)
         tile = tile.T.astype(jnp.bfloat16)
         for k in range(TILE // PAIR):
@@ -271,58 +263,56 @@
         else:
             maxima[g], totals[g], running[g] = top, total, both
 
-    def attend_local(start, stop):
-        @pl.loop(start, stop)
-        def _(g):
+    def attend_local(span):
+        for g in span:
             for part in range(2):
                 to_sibling(g, part).wait_recv()
+        for g in span:
             attend(g, 0, 2, True, chips == 1)
 
-    def attend_remote(g, together):
+    def attend_remote(span, together):
         for j in range(1, chips):
+            final = j == chips - 1
             if not together:
-                attend(g, 2 * j, 1, False, False)
-            for part in range(2):
-                forward(j, g, part).wait_recv()
-            if together:
-                attend(g, 2 * j, 2, False, j == chips - 1)
-            else:
-                attend(g, 2 * j + 1, 1, False, j == chips - 1)
-
-    advance(0)
-    attend_local(0, pairs // 2)
-    advance(1)
-    attend_local(pairs // 2, pairs)
-    advance(2)
+                for g in span:
+                    attend(g, 2 * j, 1, False, False)
+            for g in span:
+                for part in range(2):
+                    forward(j, g, part).wait_recv()
+            for g in span:
+                if together:
+                    attend(g, 2 * j, 2, False, final)
+                else:
+                    attend(g, 2 * j + 1, 1, False, final)
+
     last = TILE // PAIR
     early = qw - TILE
-
-    @pl.loop(0, 3)
-    def _(g):
-        attend_remote(g, True)
-
-    @pl.loop(3, pairs - last)
-    def _(g):
+    half = pairs // 2
+    advance(0)
+    attend_local(range(half))
+    advance(1)
+    attend_local(range(half, pairs))
+    advance(2)
+    attend_remote(range(half), True)
+    for g in range(half, pairs - last):
         advance(g)
-        attend_remote(g, False)
+        attend_remote([g], False)
 
     for load in loads[6:]:
         load.wait()
     wf_rows[...] = flip(wf[...])
 
-    @pl.loop(0, width // TILE)
-    def _(i):
-        at = pl.ds(pl.multiple_of(i * TILE, TILE), TILE)
+    for i in range(width // TILE):
+        at = pl.ds(i * TILE, TILE)
         tile = jnp.dot(
             attention[:, pl.ds(0, early)], wo[pl.ds(0, early), at],
             preferred_element_type=jnp.float32,
         )
         combined[:, at] = hidden[:, at].astype(jnp.float32) + gate[:, at] * tile
 
-    @pl.loop(pairs - last, pairs)
-    def _(g):
+    for g in range(pairs - last, pairs):
         advance(g)
-        attend_remote(g, False)
+        attend_remote([g], False)
 
     for i in range(width // TILE):
         at = pl.ds(i * TILE, TILE)
@@ -366,6 +356,7 @@
         for part in range(2):
             to_sibling(g, part).wait_send()
             for j in range(1, chips):
+                to_peer(j, g, part).wait_send()
                 forward(j, g, part).wait_send()
 
     keep.wait()

time: 29.5 us -> 29 us (0.983)
  Pallas kernels: 28 us -> 27.3 us
    pallas_call x1, Pallas kernels: 28 us -> 27.3 us  [on_device(): pl.pallas_call(functools.partial(kernel, windows, frame_devs), out_shape=...]
where the time goes in v6:
time: 29 us; the launch traced here: 28.6 us
  Pallas kernels  27.3 us (94%)
  between operations  0.67 us (2%)
  other arithmetic  0.66 us (2%)
    pallas_call x1, Pallas kernels, on_device(): pl.pallas_call(functools.partial(kernel, windows, frame_devs), out_shape=...  27.3 us
    transpose x1, other arithmetic, on_device(): return blended.T  0.65 us

profile of v6, /device:TPU:21, one launch (start us, length us, event | category | flops | bytes accessed | tf_op | source)
XLA Modules:
  0.0 28.6 jit_solution(11394293047191038527)
XLA Ops:
  0.7 27.3 %dit_window_step.1 = (f32[64,256]{1,0:T(8,128)S(1)}, bf16[64,256]{1,0:T(8,128)(2,1)S(1)}) custom-call(f32[1]{0:T(128)S(6)} %copy.12.step_hbm, bf16[256,1536]{1,0:T(8,128)(2,1)} %hidden_hbm.1, f32[64,256]{1,0:T(8,128)} %bitcast.5, bf16[256,1536]{1,0:T(8,128)(2,1)} %stale_hbm.1, f32[1,1536]{1,0:T(1,128)} %shift_hbm.1, f32[1,1536]{1,0:T(1,128)} %scale_hbm.1, ...), custom_call_target="tpu_custom_call" | custom-call | tf_op jit(solution)/shard_map/dit_window_step/pallas_call | solution.py:391
  27.9 0.6 %select_bitcast_fusion = f32[256,64]{0,1:T(8,128)} fusion(f32[64,256]{1,0:T(8,128)S(1)} %get-tuple-element.7, bf16[64,256]{1,0:T(8,128)(2,1)S(1)} %get-tuple-element.8, f32[256]{0:T(256)S(1)} %get-tuple-element.10, f32[256]{0:T(256)S(1)} %get-tuple-element.9, pred[]{:T(512)S(6)} %select_n.23), kind=kLoop, calls=%fused_computation | loop fusion | flops 81920 | bytes 165889 | tf_op jit(solution)/shard_map/transpose | solution.py:460
  (1 shorter events, 0.0 us)

commit v7 on v6

--- a/solution.py
+++ b/solution.py
@@ -8,7 +8,7 @@
 from jax.sharding import PartitionSpec as P
 
 HEAD_DIM = 64
-AHEAD = 4
+AHEAD = 6
 PAIR = 2 * HEAD_DIM
 TILE = 256
 LN_ROWS = 64

time: 29 us -> 29 us (level)
  no operation moved by 1% of the time
where the time goes in v7:
time: 29 us; the launch traced here: 28.6 us
  Pallas kernels  27.3 us (94%)
  between operations  0.67 us (2%)
  other arithmetic  0.66 us (2%)
    pallas_call x1, Pallas kernels, on_device(): pl.pallas_call(functools.partial(kernel, windows, frame_devs), out_shape=...  27.3 us
    transpose x1, other arithmetic, on_device(): return blended.T  0.65 us

profile of v7, /device:TPU:21, one launch (start us, length us, event | category | flops | bytes accessed | tf_op | source)
XLA Modules:
  0.0 28.6 jit_solution(15374347000362016564)
XLA Ops:
  0.7 27.3 %dit_window_step.1 = (f32[64,256]{1,0:T(8,128)S(1)}, bf16[64,256]{1,0:T(8,128)(2,1)S(1)}) custom-call(f32[1]{0:T(128)S(6)} %copy.12.step_hbm, bf16[256,1536]{1,0:T(8,128)(2,1)} %hidden_hbm.1, f32[64,256]{1,0:T(8,128)} %bitcast.5, bf16[256,1536]{1,0:T(8,128)(2,1)} %stale_hbm.1, f32[1,1536]{1,0:T(1,128)} %shift_hbm.1, f32[1,1536]{1,0:T(1,128)} %scale_hbm.1, ...), custom_call_target="tpu_custom_call" | custom-call | tf_op jit(solution)/shard_map/dit_window_step/pallas_call | solution.py:391
  27.9 0.6 %select_bitcast_fusion = f32[256,64]{0,1:T(8,128)} fusion(f32[64,256]{1,0:T(8,128)S(1)} %get-tuple-element.7, bf16[64,256]{1,0:T(8,128)(2,1)S(1)} %get-tuple-element.8, f32[256]{0:T(256)S(1)} %get-tuple-element.10, f32[256]{0:T(256)S(1)} %get-tuple-element.9, pred[]{:T(512)S(6)} %select_n.23), kind=kLoop, calls=%fused_computation | loop fusion | flops 81920 | bytes 165889 | tf_op jit(solution)/shard_map/transpose | solution.py:460
  (1 shorter events, 0.0 us)
